TPU v7x, 256 devices: a whole 4x4x8 slice. The times are simulated.
256 devices in a mesh: fam: 8 (over y_hi, x), owner: 32 (over y_lo, z, core).
Axes of the slice: x: 4, y: 4 (y_hi: 2, y_lo: 2; y = y_hi * 2 + y_lo), z: 8, core: 2. Of those that a mesh axis runs over, the one named last changes fastest.
Arguments:
- wavefunction: bfloat16 [16384, 512], P('owner'), may hold values from -6 to 6
- left_blocks: bfloat16 [8, 8, 16384, 1024], P('fam', None, 'owner'), may hold values from -0.1875 to 0.1875
- right_blocks: bfloat16 [8, 512, 512], P('fam'), may hold values from -0.0625 to 0.0625
- term_sources: int32 [8, 16, 8], replicated, may hold values from 0 to 15
- term_counts: int32 [8, 16], replicated, may hold values from 1 to 8, as said below
- sector_rows: int32 [16], replicated, may hold values from 256 to 1024
Outputs:
- sigma: bfloat16 [16384, 512], P('owner', 'fam')
Inputs may be any that keep to these rules, and one draw needn't show every extreme that they name: `term_counts`: every entry lies in 1 to 8; for every output sector some family has exactly 8 live slots.
All inputs are finite; a program needn't handle non-finite values.
Results may differ from a plain program's by a relative error of at most 0.0095.
Values may be sent and summed in bfloat16 or wider, within the bound.
A program may use at most 128 MiB of HBM per device.

v0:
```python
import jax
import jax.numpy as jnp
from jax import lax
from jax.sharding import PartitionSpec as P


def in_blocks(value, dim, count):
    dims = value.shape
    parts = value.reshape(*dims[:dim], count, dims[dim] // count, *dims[dim + 1 :])
    return jnp.moveaxis(parts, dim, 0)


def sent_and_summed(value, axis, dim):
    count = lax.axis_size(axis)
    parts = lax.all_to_all(in_blocks(value, dim, count), axis, 0, 0, tiled=True)
    return jnp.sum(parts, axis=0)


def row_keep(global_rows, sector_len, sector_rows):
    sector = global_rows // sector_len
    table = jnp.arange(sector_rows.shape[0], dtype=jnp.int32)
    used = jnp.sum(jnp.where(sector[:, None] == table[None, :], sector_rows[None, :], 0), axis=1)
    return global_rows % sector_len < used


def body(wavefunction, left_blocks, right_blocks, term_sources, term_counts, sector_rows):
    rows_dev, columns = wavefunction.shape
    slot_count = left_blocks.shape[1]
    sector_len = left_blocks.shape[3]
    fam_here = lax.axis_index("fam")
    first_row = lax.axis_index("owner") * rows_dev
    global_rows = first_row + jnp.arange(rows_dev, dtype=jnp.int32)
    keep = row_keep(global_rows, sector_len, sector_rows)
    masked = jnp.where(keep[:, None], wavefunction, jnp.zeros_like(wavefunction))
    out_sector = [(first_row + 0) // sector_len]
    slot_ids = jnp.arange(slot_count, dtype=jnp.int32)
    items = left_blocks[0]
    right_stack = right_blocks[0]
    block = 0
    live = [slot_ids < term_counts[fam_here, out_sector[block]]]
    source = term_sources[fam_here, out_sector[block], slot_ids]
    whole = lax.all_gather(masked, "owner", axis=0, tiled=True)
    stacked = whole.reshape(whole.shape[0] // sector_len, sector_len, whole.shape[1])
    sources = jnp.take(stacked, source, axis=0)
    accum = jnp.stack(
        [jnp.einsum("kri,kic->krc", items, sources, preferred_element_type=jnp.float32)], axis=0
    )
    partial_value = accum.astype(jnp.bfloat16)
    block = 0
    used = jnp.where(
        live[block][:, None, None], partial_value[block], jnp.zeros_like(partial_value[block])
    )
    total = jnp.einsum("krc,cd->rd", used, right_stack, preferred_element_type=jnp.float32)
    combined = total
    combined = jnp.where(keep[:, None], combined, jnp.zeros_like(combined))
    summed = sent_and_summed(combined, "fam", 1)
    return summed.astype(jnp.bfloat16)


def solution(mesh):
    return jax.shard_map(
        body,
        mesh=mesh,
        in_specs=(
            P("owner", None),
            P("fam", None, "owner", None),
            P("fam", None, None),
            P(),
            P(),
            P(),
        ),
        out_specs=P("owner", "fam"),
        check_vma=False,
    )
```

profile of v0, /device:TPU:1, one launch (start us, length us, event | category | flops | bytes accessed | tf_op | source)
XLA Modules:
  0.0 180.4 jit_solution(4787722068686721112)
XLA Ops:
  6.5 0.0 copy-start
  6.5 0.0 all-gather.2.cloned.1.call-start
  6.5 1.3 copy.10
  7.9 0.7 select_reduce_fusion
  8.6 0.8 broadcast_select_fusion
  9.5 0.0 all-gather.2.cloned.1.call-update
  9.5 1.3 dynamic_slice.3
  10.8 1.4 gather_fusion
  12.2 0.7 compare_and_fusion
  12.9 100.7 %all-gather.2.cloned.1.call-done = bf16[16384,512]{0,1:T(8,128)(2,1)} async-done(((bf16[512,512]{0,1:T(8,128)(2,1)}), bf16[16384,512]{0,1:T(8,128)(2,1)}) %all-gather.2.cloned.1.call-update) | async-done | bytes 16777232 | tf_op jit(solution)/shard_map/all_gather | solution.py:42
  113.6 14.0 %copy.14 = bf16[64,16,8,1024]{3,2,0,1:T(8,128)(2,1)} copy(bf16[64,16,8,1024]{3,2,1,0:T(8,128)(2,1)} %bitcast.24) | data formatting | bytes 33554432 | tf_op jit(solution)/shard_map/reshape | solution.py:43
  127.6 10.4 %gather_fusion.1 = bf16[8,1024,512]{1,2,0:T(8,128)(2,1)} fusion(bf16[16,1024,512]{1,2,0:T(8,128)(2,1)} %bitcast.23, s32[1024]{0:T(1024)S(1)} %pad_clamp_fusion), kind=kCustom, calls=%fused_computation.1 | custom fusion | bytes 16777248 | tf_op jit(solution)/shard_map/jit(_take)/gather | solution.py:44
  138.1 10.7 %convert_reduce_fusion = bf16[512,512]{1,0:T(8,128)(2,1)S(1)} fusion(pred[8]{0:T(512)(128)(4,1)S(1)} %get-tuple-element.6, bf16[1,8,512,1024]{3,2,1,0:T(8,128)(2,1)} %param.7, bf16[8,1024,512]{1,2,0:T(8,128)(2,1)} %gather_fusion.1, pred[8]{0:T(512)(128)(4,1)S(1)} %get-tuple-element.5), kind=kOutput, calls=%fused_computation.5 | convolution fusion | flops 4307288064 | bytes 17301520 | tf_op jit(solution)/shard_map/kri,kic->krc/dot_general | solution.py:46
  148.8 0.0 copy-done
  148.8 0.5 convolution_select_fusion
  149.3 23.6 %all_to_all.5 = f32[8,512,64]{1,2,0:T(8,128)S(1)} all-to-all(f32[8,512,64]{1,2,0:T(8,128)S(1)} %bitcast.25), channel_id=1, replica_groups=mesh['fam'=8,'owner'=32] {'fam'}, dimensions={0} | all-to-all | bytes 2097152 | tf_op jit(solution)/shard_map/all_to_all | solution.py:15
  172.9 0.7 reduce_sum.29
  (5 shorter events, 0.0 us)
Async XLA Ops:
  6.5 142.3 %copy-start = (bf16[1,512,512]{2,1,0:T(8,128)(2,1)S(1)}, bf16[1,512,512]{2,1,0:T(8,128)(2,1)}, u32[]{:S(2)}) copy-start(bf16[1,512,512]{2,1,0:T(8,128)(2,1)} %param.8) | copy-start | bytes 1572868
  6.5 107.1 %all-gather.2.cloned.1.call-start = ((), (), s32[]{:S(2)}) async-start(), calls=%async_computation.1 | async-start | bytes 17301504 | tf_op jit(solution)/shard_map/all_gather | solution.py:42
Sparse Core Ops, SparseCore 0:
  9.6 103.9 all-gather.1
where the time goes:
time: 181 us; the launch traced here: 180 us
  waiting for transfers between devices  101 us (56%)
  local copies, waits for them, and re-layouts  28.4 us (16%)
  blocking collectives  23.6 us (13%)
  between operations  13.5 us (7%)
  matrix products  11.2 us (6%)
  other arithmetic  2.99 us (2%)
    all_gather x1, waiting for transfers between devices, body(): whole = lax.all_gather(masked, 'owner', axis=0, tiled=True)  101 us
    all_to_all x1, blocking collectives, sent_and_summed(): parts = lax.all_to_all(in_blocks(value, dim, count), axis, 0, 0, tiled=True)  23.6 us
    reshape x1, local copies, waits for them, and re-layouts, body(): whole.reshape(whole.shape[0] // sector_len, sector_len, whole.shape[1])  14 us
    dot_general x1, matrix products, body(): jnp.einsum('kri,kic->krc', items, sources, preferred_element_type=jnp.flo...  10.7 us
    gather x1, local copies, waits for them, and re-layouts, body(): sources = jnp.take(stacked, source, axis=0)  10.4 us
  transfers between devices with their start and end apart: 1, of which 1 were waited for; matrix products, arithmetic and copies ran while one was open for 2% of the time, Pallas kernels for 0%

commit v1 on v0

--- a/solution.py
+++ b/solution.py
@@ -39,7 +39,8 @@
     block = 0
     live = [slot_ids < term_counts[fam_here, out_sector[block]]]
     source = term_sources[fam_here, out_sector[block], slot_ids]
-    whole = lax.all_gather(masked, "owner", axis=0, tiled=True)
+    sent = jnp.stack([masked] * lax.axis_size("owner"))
+    whole = jnp.concatenate(lax.all_to_all(sent, "owner", 0, 0), axis=0)
     stacked = whole.reshape(whole.shape[0] // sector_len, sector_len, whole.shape[1])
     sources = jnp.take(stacked, source, axis=0)
     accum = jnp.stack(

time: 181 us -> 436 us (2.41)
  the two profiles are of different devices: /device:TPU:1 before, /device:TPU:96 now
where the time goes in v1:
time: 436 us
  waiting for transfers between devices  371 us (85%)
  blocking collectives  23.4 us (5%)
  local copies, waits for them, and re-layouts  19.9 us (5%)
  matrix products  10.7 us (2%)
  starting transfers between devices  9.02 us (2%)
    all_to_all x1, waiting for transfers between devices, body(): whole = jnp.concatenate(lax.all_to_all(sent, 'owner', 0, 0), axis=0)  371 us
    all_to_all x1, blocking collectives, sent_and_summed(): parts = lax.all_to_all(in_blocks(value, dim, count), axis, 0, 0, tiled=True)  23.4 us
    gather x1, local copies, waits for them, and re-layouts, body(): sources = jnp.take(stacked, source, axis=0)  10.4 us
    dot_general x1, matrix products, body(): jnp.einsum('kri,kic->krc', items, sources, preferred_element_type=jnp.flo...  10.2 us
    all_to_all x1, starting transfers between devices, body(): whole = jnp.concatenate(lax.all_to_all(sent, 'owner', 0, 0), axis=0)  9.02 us
  transfers between devices with their start and end apart: 1, of which 1 were waited for; matrix products, arithmetic and copies ran while one was open for 1% of the time, Pallas kernels for 0%

profile of v1, /device:TPU:96, one launch (start us, length us, event | category | flops | bytes accessed | tf_op | source)
XLA Modules:
  0.0 435.9 jit_solution(16040021069954372621)
XLA Ops:
  0.0 0.0 copy-start
  0.0 1.3 copy.13
  1.3 0.7 select_reduce_fusion
  2.1 0.2 copy.14
  2.4 6.0 %stack.2 = bf16[32,512,512]{2,1,0:T(8,128)(2,1)} broadcast(bf16[512,512]{1,0:T(8,128)(2,1)S(1)} %copy.14), dimensions={1,2} | broadcast | bytes 17301504 | tf_op jit(solution)/shard_map/stack | solution.py:42
  8.3 0.0 copy-start.1
  8.3 9.0 %all-to-all-start = ((bf16[32,512,512]{2,1,0:T(8,128)(2,1)}), bf16[32,512,512]{2,1,0:T(8,128)(2,1)}, u32[]{:S(2)}, u32[]{:S(2)}) async-start(bf16[32,512,512]{2,1,0:T(8,128)(2,1)} %stack.2), calls=%async_computation | async-start | bytes 33554432 | tf_op jit(solution)/shard_map/all_to_all | solution.py:43
  17.4 1.3 dynamic_slice.3
  18.7 0.0 copy-done.1
  18.7 0.6 gather_fusion
  19.3 0.7 compare_and_fusion
  20.0 370.6 %all-to-all-done = bf16[32,512,512]{2,1,0:T(8,128)(2,1)} async-done(((bf16[32,512,512]{2,1,0:T(8,128)(2,1)}), bf16[32,512,512]{2,1,0:T(8,128)(2,1)}, u32[]{:S(2)}, u32[]{:S(2)}) %all-to-all-start) | async-done | bytes 16777248 | tf_op jit(solution)/shard_map/all_to_all | solution.py:43
  390.6 10.4 %gather_fusion.1 = bf16[8,1024,512]{2,1,0:T(8,128)(2,1)} fusion(bf16[16,1024,512]{2,1,0:T(8,128)(2,1)} %bitcast.2, s32[1024]{0:T(1024)S(1)} %pad_clamp_fusion), kind=kCustom, calls=%fused_computation.1 | custom fusion | bytes 16777248 | tf_op jit(solution)/shard_map/jit(_take)/gather | solution.py:45
  401.0 10.2 %convert_reduce_fusion = bf16[512,512]{1,0:T(8,128)(2,1)S(1)} fusion(pred[8]{0:T(512)(128)(4,1)S(1)} %get-tuple-element.6, bf16[1,8,512,1024]{3,2,1,0:T(8,128)(2,1)} %param.7, bf16[8,1024,512]{2,1,0:T(8,128)(2,1)} %gather_fusion.1, pred[8]{0:T(512)(128)(4,1)S(1)} %get-tuple-element.5), kind=kOutput, calls=%fused_computation.4 | convolution fusion | flops 4307288064 | bytes 17301520 | tf_op jit(solution)/shard_map/kri,kic->krc/dot_general | solution.py:47
  411.2 0.0 copy-done
  411.2 0.5 convolution_select_fusion
  411.7 23.4 %all_to_all.10 = f32[8,512,64]{1,2,0:T(8,128)S(1)} all-to-all(f32[8,512,64]{1,2,0:T(8,128)S(1)} %bitcast.20), channel_id=1, replica_groups=mesh['fam'=8,'owner'=32] {'fam'}, dimensions={0} | all-to-all | bytes 2097152 | tf_op jit(solution)/shard_map/all_to_all | solution.py:15
  435.2 0.7 reduce_sum.29
  (6 shorter events, 0.1 us)
Async XLA Ops:
  0.0 411.2 %copy-start = (bf16[1,512,512]{2,1,0:T(8,128)(2,1)S(1)}, bf16[1,512,512]{2,1,0:T(8,128)(2,1)}, u32[]{:S(2)}) copy-start(bf16[1,512,512]{2,1,0:T(8,128)(2,1)} %param.8) | copy-start | bytes 1572868
  8.3 10.3 %copy-start.1 = (s32[8,16,8]{1,2,0:T(8,128)S(1)}, s32[8,16,8]{1,2,0:T(8,128)}, u32[]{:S(2)}) copy-start(s32[8,16,8]{1,2,0:T(8,128)} %param.9) | copy-start | bytes 12292
  8.3 382.2 %all-to-all-start = ((bf16[32,512,512]{2,1,0:T(8,128)(2,1)}), bf16[32,512,512]{2,1,0:T(8,128)(2,1)}, u32[]{:S(2)}, u32[]{:S(2)}) async-start(bf16[32,512,512]{2,1,0:T(8,128)(2,1)} %stack.2), calls=%async_computation | async-start | bytes 33554432 | tf_op jit(solution)/shard_map/all_to_all | solution.py:43
